TPU v7x, 256 devices: a whole 4x4x8 slice. The times are simulated.
256 devices in a mesh: ctx: 64 (over z, y_lo, x), tp: 4 (over y_hi, core).
Axes of the slice: x: 4, y: 4 (y_hi: 2, y_lo: 2; y = y_hi * 2 + y_lo), z: 8, core: 2. Of those that a mesh axis runs over, the one named last changes fastest.
Arguments:
- queries: bfloat16 [512, 4096], P('ctx', 'tp'), may hold values from -48 to 48
- suffix_keys: bfloat16 [512, 1024], P('ctx', 'tp'), may hold values from -12 to 12
- suffix_values: bfloat16 [512, 1024], P('ctx', 'tp'), may hold values from -6 to 6
- prefix_keys: bfloat16 [262144, 1024], P('ctx', 'tp'), may hold values from -6 to 6
- prefix_values: bfloat16 [262144, 1024], P('ctx', 'tp'), may hold values from -6 to 6
- lengths: int32 [8], replicated, may hold values from 1 to 64, 384 in all
- parents: int32 [8], replicated, may hold values from 0 to 7, as said below
- out_weight: bfloat16 [4096, 4096], P('tp', 'ctx'), may hold values from -0.5 to 0.5
- residual: bfloat16 [512, 4096], P('tp', 'ctx'), may hold values from -6 to 6
Outputs:
- layer_state: bfloat16 [512, 4096], P('tp', 'ctx')
Inputs may be any that keep to these rules, and one draw needn't show every extreme that they name: parents[j] <= j; parents[j] == j marks a leaf that follows the prefix directly.
All inputs are finite; a program needn't handle non-finite values.
Results may differ from a plain program's by a relative error of at most 0.006.
Values may be sent and summed in bfloat16 or wider, within the bound.
A program may use at most 320 MiB of HBM per device.

v0:
```python
import math

import jax
import jax.numpy as jnp
from jax import lax
from jax.sharding import PartitionSpec as P

HD = 128


def ancestry(parents):
    leaf_count = parents.shape[0]
    leaf_ids = jnp.arange(leaf_count, dtype=jnp.int32)
    current = leaf_ids
    ancestors = jnp.zeros((leaf_count, leaf_count), jnp.int32)
    for hop_index in range(leaf_count):
        following = jnp.sum(
            jnp.where(current[:, None] == leaf_ids[None, :], parents[None, :], 0), axis=1
        )
        new_links = (leaf_ids[None, :] == following[:, None]) & (following != current)[:, None]
        ancestors = jnp.maximum(ancestors, new_links.astype(jnp.int32))
        current = following
    return ancestors


def visible(row_ids, lengths, parents, token_count):
    leaf_count = lengths.shape[0]
    leaf_span = token_count // leaf_count
    leaf_ids = jnp.arange(leaf_count, dtype=jnp.int32)
    key_ids = jnp.arange(token_count, dtype=jnp.int32)
    key_leaf = key_ids // leaf_span
    key_place = key_ids % leaf_span
    row_leaf = row_ids // leaf_span
    row_place = row_ids % leaf_span
    live_keys = key_place < jnp.repeat(lengths, leaf_span)
    onehot = (row_leaf[:, None] == leaf_ids[None, :]).astype(jnp.int32)
    elders = jnp.repeat(jnp.dot(onehot, ancestry(parents)), leaf_span, axis=1) > 0
    own_leaf = (row_leaf[:, None] == key_leaf[None, :]) & (key_place[None, :] <= row_place[:, None])
    return live_keys[None, :] & (elders | own_leaf)


def shards(
    queries,
    suffix_keys,
    suffix_values,
    prefix_keys,
    prefix_values,
    lengths,
    parents,
    out_weight,
    residual,
):
    inverse_root = 1.0 / math.sqrt(HD)
    all_queries, all_keys, all_values = (
        lax.all_gather(queries, "ctx", axis=0, tiled=True),
        lax.all_gather(suffix_keys, "ctx", axis=0, tiled=True),
        lax.all_gather(suffix_values, "ctx", axis=0, tiled=True),
    )
    token_count = all_queries.shape[0]
    groups = all_keys.shape[1] // HD
    per_group = all_queries.shape[1] // HD // groups
    query_rows = min(64, token_count)
    query_blocks = all_queries.reshape(token_count // query_rows, query_rows, groups, per_group, HD)
    key_table = prefix_keys.reshape(prefix_keys.shape[0], groups, HD)
    value_table = prefix_values.reshape(prefix_values.shape[0], groups, HD)

    def prefix_block(query_block):
        scores = (
            jnp.einsum("bgrd,kgd->bgrk", query_block, key_table, preferred_element_type=jnp.float32)
            * inverse_root
        )
        block_peak = jnp.max(scores, axis=-1)
        weights = jnp.exp(scores - block_peak[..., None]).astype(jnp.bfloat16)
        block_total = jnp.sum(weights, axis=-1, dtype=jnp.float32)
        block_sum = jnp.einsum(
            "bgrk,kgd->bgrd", weights, value_table, preferred_element_type=jnp.float32
        )
        return (block_peak, block_total, block_sum)

    block_peaks, totals, weighted = lax.map(prefix_block, query_blocks)
    block_peaks = block_peaks.reshape(token_count, groups, per_group)
    totals = totals.reshape(token_count, groups, per_group)
    weighted = weighted.reshape(token_count, groups, per_group, HD)
    highest = lax.pmax(block_peaks, "ctx")
    factor = jnp.exp(block_peaks - highest)
    totals = totals * factor
    weighted = weighted * factor[..., None]
    totals, weighted = lax.psum((totals, weighted), "ctx")
    row_ids = jnp.arange(token_count, dtype=jnp.int32)
    row_queries = all_queries.reshape(token_count, groups, per_group, HD)
    allowed = visible(row_ids, lengths, parents, token_count)[:, None, None, :]
    leaf_keys = all_keys.reshape(token_count, groups, HD)
    leaf_vals = all_values.reshape(token_count, groups, HD)
    leaf_scores = (
        jnp.einsum("qgrd,kgd->qgrk", row_queries, leaf_keys, preferred_element_type=jnp.float32)
        * inverse_root
    )
    leaf_peak = jnp.max(jnp.where(allowed, leaf_scores, -jnp.inf), axis=-1)
    leaf_weight = jnp.where(allowed, jnp.exp(leaf_scores - leaf_peak[..., None]), 0.0).astype(
        jnp.bfloat16
    )
    leaf_total = jnp.sum(leaf_weight, axis=-1, dtype=jnp.float32)
    leaf_sum = jnp.einsum(
        "qgrk,kgd->qgrd", leaf_weight, leaf_vals, preferred_element_type=jnp.float32
    )
    joined_peak = jnp.maximum(highest, leaf_peak)
    prefix_scale = jnp.exp(highest - joined_peak)
    leaf_scale = jnp.exp(leaf_peak - joined_peak)
    numerator = weighted * prefix_scale[..., None] + leaf_sum * leaf_scale[..., None]
    denominator = totals * prefix_scale + leaf_total * leaf_scale
    attention = (
        (numerator / denominator[..., None])
        .reshape(token_count, groups * per_group * HD)
        .astype(jnp.bfloat16)
    )
    projected = jnp.dot(attention, out_weight, preferred_element_type=jnp.float32)
    shares = lax.psum_scatter(projected, "tp", scatter_dimension=0, tiled=True)
    return (residual.astype(jnp.float32) + shares).astype(jnp.bfloat16)


def solution(mesh):
    placed = (
        P("ctx", "tp"),
        P("ctx", "tp"),
        P("ctx", "tp"),
        P("ctx", "tp"),
        P("ctx", "tp"),
        P(),
        P(),
        P("tp", "ctx"),
        P("tp", "ctx"),
    )
    return jax.shard_map(
        shards, mesh=mesh, in_specs=placed, out_specs=P("tp", "ctx"), check_vma=False
    )
```

profile of v0, /device:TPU:1, one launch (start us, length us, event | category | flops | bytes accessed | tf_op | source)
XLA Modules:
  0.0 1453.0 jit_solution(5015347217559304092)
XLA Ops:
  7.3 4.1 copy.44
  11.5 3.1 copy.47
  14.6 4.1 copy.45
  18.8 4.1 copy.48
  22.9 134.7 %all_gather.11 = bf16[512,256]{1,0:T(8,128)(2,1)S(1)} all-gather(bf16[8,256]{1,0:T(8,128)(2,1)S(1)} %copy-done.7), channel_id=1, replica_groups=mesh['ctx'=64,'tp'=4] {'ctx'}, dimensions={0}, use_global_device_ids=true | all-gather | bytes 266240 | tf_op jit(solution)/shard_map/all_gather | solution.py:57
  158.6 125.6 %all_gather.10 = bf16[512,256]{1,0:T(8,128)(2,1)S(1)} all-gather(bf16[8,256]{1,0:T(8,128)(2,1)S(1)} %copy-done.8), channel_id=1, replica_groups=mesh['ctx'=64,'tp'=4] {'ctx'}, dimensions={0}, use_global_device_ids=true | all-gather | bytes 266240 | tf_op jit(solution)/shard_map/all_gather | solution.py:56
  286.3 1.8 reshape.207
  288.1 148.4 %while.14 = (s32[]{:T(128)}, f32[8,64,2,4]{1,0,3,2:T(8,128)}, f32[8,64,2,4]{1,0,3,2:T(8,128)}, f32[8,64,2,4,128]{4,1,0,3,2:T(8,128)}, bf16[8,64,2,4,128]{4,3,2,1...) while((s32[]{:T(128)}, f32[8,64,2,4]{1,0,3,2:T(8,128)}, ...), condition=%wide.region_3.4_spmd, body=%wide.region_0.3_spmd.sunk | while | flops 1094712320 | bytes 30031988 | solution.py:80
  288.2 4.5 bitcast_reduce_fusion.2
  294.0 4.9 convert_reduce_fusion.3
  300.3 6.4 fusion.96
  306.7 4.5 bitcast_reduce_fusion.2
  312.6 4.9 convert_reduce_fusion.3
  317.5 1.4 dynamic_update_slice.17
  318.9 6.4 fusion.96
  325.3 4.5 bitcast_reduce_fusion.2
  331.1 4.9 convert_reduce_fusion.3
  336.0 1.4 dynamic_update_slice.17
  337.4 6.4 fusion.96
  343.9 4.5 bitcast_reduce_fusion.2
  349.7 4.9 convert_reduce_fusion.3
  354.6 1.4 dynamic_update_slice.17
  356.0 6.4 fusion.96
  362.4 4.5 bitcast_reduce_fusion.2
  368.3 4.9 convert_reduce_fusion.3
  373.1 1.4 dynamic_update_slice.17
  374.5 6.4 fusion.96
  380.9 4.5 bitcast_reduce_fusion.2
  386.8 4.9 convert_reduce_fusion.3
  393.1 6.4 fusion.96
  399.5 4.5 bitcast_reduce_fusion.2
  405.3 4.9 convert_reduce_fusion.3
  411.6 6.4 fusion.96
  418.1 4.5 bitcast_reduce_fusion.2
  423.9 4.9 convert_reduce_fusion.3
  430.2 6.4 fusion.96
  436.6 1.9 copy.51
  438.5 1.5 reshape.216
  440.0 1.4 reshape.211
  441.4 249.2 %pmax.7 = f32[512,2,4]{0,2,1:T(4,128)} all-reduce(f32[512,2,4]{0,2,1:T(4,128)} %reshape.211), channel_id=1, replica_groups=mesh['ctx'=64,'tp'=4] {'ctx'}, use_global_device_ids=true, to_apply=%region_4.5 | all-reduce | flops 4096 | bytes 32768 | tf_op jit(solution)/shard_map/pmax | solution.py:84
  692.0 1.6 broadcast_multiply_fusion
  696.4 249.3 %psum.15 = f32[512,2,4]{0,2,1:T(4,128)S(1)} all-reduce(f32[512,2,4]{0,2,1:T(4,128)S(1)} %bitcast.145), channel_id=1, replica_groups=mesh['ctx'=64,'tp'=4] {'ctx'}, use_global_device_ids=true, to_apply=%region_15.16 | all-reduce | flops 4096 | bytes 32768 | tf_op jit(solution)/shard_map/psum | solution.py:88
  945.7 1.5 fusion.14
  947.3 1.8 convert_reduce_fusion.1
  949.0 1.4 copy-done.1
  950.5 413.1 %all-reduce.2.cloned.1.call-done = f32[512,2,4,128]{0,3,2,1:T(8,128)} async-done(((f32[512,2,4,128]{0,3,2,1:T(8,128)}), f32[512,2,4,128]{0,3,2,1:T(8,128)}) %all-reduce.2.cloned.1.call-update) | async-done | bytes 2097168 | tf_op jit(solution)/shard_map/psum | solution.py:88
  1363.6 6.1 fusion.20
  1370.7 74.4 %reduce-scatter.2.cloned.1.call-done = f32[128,64]{0,1:T(8,128)} async-done(((f32[512,64]{0,1:T(8,128)}), f32[128,64]{0,1:T(8,128)}) %reduce-scatter.2.cloned.1.call-update) | async-done | bytes 32784 | tf_op jit(solution)/shard_map/reduce_scatter | solution.py:117
  (85 shorter events, 27.3 us)
Async XLA Ops:
  6.5 1363.2 %copy-start = (bf16[1024,64]{0,1:T(8,128)(2,1)S(1)}, bf16[1024,64]{0,1:T(8,128)(2,1)}, u32[]{:S(2)}) copy-start(bf16[1024,64]{0,1:T(8,128)(2,1)} %param.18) | copy-start | bytes 393220
  6.5 279.8 %all-gather.2.cloned.1.call-start = ((), (), s32[]{:S(2)}) async-start(), calls=%async_computation.1 | async-start | bytes 1064960 | tf_op jit(solution)/shard_map/all_gather | solution.py:55
  7.3 1356.3 %all-reduce.2.cloned.1.call-start = ((), (), s32[]{:S(2)}) async-start(), calls=%async_computation.2 | async-start | bytes 4194304 | tf_op jit(solution)/shard_map/psum | solution.py:88
  14.6 8.3 copy-start.7
  14.6 143.8 %copy-start.9 = (s32[8]{0:T(128)S(1)}, s32[8]{0:T(128)}, u32[]{:S(2)}) copy-start(s32[8]{0:T(128)} %param.16) | copy-start | bytes 100
  14.6 143.9 %copy-start.8 = (bf16[8,256]{1,0:T(8,128)(2,1)S(1)}, bf16[8,256]{1,0:T(8,128)(2,1)}, u32[]{:S(2)}) copy-start(bf16[8,256]{1,0:T(8,128)(2,1)} %param.12) | copy-start | bytes 12292
  14.6 269.7 %copy-start.16 = (s32[8]{0:T(128)S(1)}, s32[8]{0:T(128)}, u32[]{:S(2)}) copy-start(s32[8]{0:T(128)} %param.17) | copy-start | bytes 100
  284.6 3.5 copy-start.10
  284.8 1.5 copy-start.11
  285.0 1.3 copy-start.12
  285.2 1.1 copy-start.13
  285.3 0.9 copy-start.14
  285.5 0.7 copy-start.15
  438.5 257.4 %copy-start.2 = (bf16[512,1024]{1,0:T(8,128)(2,1)S(1)}, bf16[512,1024]{1,0:T(8,128)(2,1)}, u32[]{:S(2)}) copy-start(bf16[512,1024]{1,0:T(8,128)(2,1)} %all-gather.2.cloned.1.call-done) | copy-start | bytes 3145732
  693.6 2.8 copy-start.5
  693.6 751.4 %reduce-scatter.2.cloned.1.call-start = ((), (), s32[]{:S(2)}) async-start(), calls=%async_computation.3 | async-start | bytes 163840 | tf_op jit(solution)/shard_map/reduce_scatter | solution.py:117
  947.2 3.2 copy-start.1
  947.2 3.2 copy-start.4
  947.3 416.3 %copy-start.3 = (bf16[512,256]{0,1:T(8,128)(2,1)S(1)}, bf16[512,256]{0,1:T(8,128)(2,1)}, u32[]{:S(2)}) copy-start(bf16[512,256]{0,1:T(8,128)(2,1)} %copy.56) | copy-start | bytes 786436
  1363.6 81.5 %copy-start.6 = (bf16[128,64]{0,1:T(8,128)(2,1)S(1)}, bf16[128,64]{0,1:T(8,128)(2,1)}, u32[]{:S(2)}) copy-start(bf16[128,64]{0,1:T(8,128)(2,1)} %param.19) | copy-start | bytes 49156
Sparse Core Ops, SparseCore 0:
  9.1 256.0 all-gather.1
  693.7 669.8 all-reduce.1
  1370.8 74.2 reduce-scatter.1
where the time goes:
time: 1460 us; the launch traced here: 1450 us
  blocking collectives  759 us (52%)
  waiting for transfers between devices  488 us (33%)
  matrix products  96.5 us (7%)
  other arithmetic  48.1 us (3%)
  local copies, waits for them, and re-layouts  47.8 us (3%)
    psum x1, waiting for transfers between devices, shards(): totals, weighted = lax.psum((totals, weighted), 'ctx')  413 us
    psum x1, blocking collectives, shards(): totals, weighted = lax.psum((totals, weighted), 'ctx')  249 us
    pmax x1, blocking collectives, shards(): highest = lax.pmax(block_peaks, 'ctx')  249 us
    all_gather x1, blocking collectives, shards(): lax.all_gather(suffix_values, 'ctx', axis=0, tiled=True)  135 us
    all_gather x1, blocking collectives, shards(): lax.all_gather(suffix_keys, 'ctx', axis=0, tiled=True)  126 us
    reduce_scatter x1, waiting for transfers between devices, shards(): shares = lax.psum_scatter(projected, 'tp', scatter_dimension=0, tiled=True)  74.4 us
    dot_general x8, matrix products, prefix_block(): jnp.einsum('bgrk,kgd->bgrd', weights, value_table, preferred_element_type...  51.1 us
    reduce_sum x8, other arithmetic, prefix_block(): block_total = jnp.sum(weights, axis=-1, dtype=jnp.float32)  39 us
  transfers between devices with their start and end apart: 3, of which 2 were waited for; matrix products, arithmetic and copies ran while one was open for 2% of the time, Pallas kernels for 0%

commit v1 on v0

v1 whole, which is shorter than its diff:
```python
import math

import jax
import jax.numpy as jnp
from jax import lax
from jax.experimental import pallas as pl
from jax.experimental.pallas import tpu as pltpu
from jax.sharding import PartitionSpec as P

HD = 128
NX, NY, NZ = 4, 2, 8
NP = NX * NY
NT = 4
LEAF_ROWS = 32
ROWS = NZ * LEAF_ROWS
TAIL = 16
KEYS = 4096
TILE = 1024
SCALE = math.log2(math.e) / math.sqrt(HD)
LOW = -1e30
F32, BF16 = jnp.float32, jnp.bfloat16
MESH = pl.DeviceIdType.MESH


def split3(x):
    hi = x.astype(BF16).astype(F32)
    rest = x - hi
    mid = rest.astype(BF16).astype(F32)
    low = (rest - mid).astype(BF16).astype(F32)
    return hi, mid, low


def pack_tail(lam):
    zeros = jnp.zeros((TAIL - 6, 128), F32)
    return jnp.concatenate([*split3(lam), zeros], axis=0).astype(BF16)


def read_tail(tail):
    tail = tail.astype(F32)
    return tail[0:2] + tail[2:4] + tail[4:6]


def kernel(
    lengths, parents, q_in, sk_in, sv_in, pk_hbm, pv_hbm, w_in, res_in, out_ref,
    keys, values, sk, sv, anc, w2, q, sums, recv_a, part_b, recv_b, att, proj, recv_p,
    load_sem, qz_s, qz_r, qp_s, qp_r, a_s, a_r, b_s, b_r, gz_s, gz_r, gp_s, gp_r, t_s, t_r,
):
    c, t = lax.axis_index("ctx"), lax.axis_index("tp")
    z, p = c // NP, c % NP
    y, x = p // NX, p % NX

    def plane(j, sign):
        xx = (x + NX + sign * (j % NX)) % NX
        yy = (y + NY + sign * (j // NX)) % NY
        return yy * NX + xx

    def at_z(k, sign):
        return (z + NZ + sign * k) % NZ

    def remote(src, dst, send, recv, ctx, tp):
        return pltpu.make_async_remote_copy(
            src_ref=src, dst_ref=dst, send_sem=send, recv_sem=recv,
            device_id=(ctx, tp), device_id_type=MESH,
        )

    loads = []
    for g in range(2):
        cols = pl.ds(g * HD, HD)
        loads.append(pltpu.make_async_copy(pk_hbm.at[:, cols], keys.at[g], load_sem.at[2 * g]))
        loads.append(pltpu.make_async_copy(pv_hbm.at[:, cols], values.at[g], load_sem.at[2 * g + 1]))
    for load in loads:
        load.start()

    barrier = pltpu.get_barrier_semaphore()
    for k in range(1, NZ):
        pl.semaphore_signal(barrier, inc=1, device_id=(at_z(k, 1) * NP + p, t), device_id_type=MESH)
    for j in range(1, NP):
        pl.semaphore_signal(barrier, inc=1, device_id=(z * NP + plane(j, 1), t), device_id_type=MESH)
    for k in range(1, NT):
        pl.semaphore_signal(barrier, inc=1, device_id=(c, (t + k) % NT), device_id_type=MESH)

    own = q_in[...].astype(F32)
    for g in range(2):
        heads = [own[:, (4 * g + h) * HD : (4 * g + h + 1) * HD] for h in range(4)]
        q[g, p, z] = jnp.concatenate(heads, axis=0).astype(BF16)
    pl.semaphore_wait(barrier, NZ - 1 + NP - 1 + NT - 1)

    def q_z(g, k):
        block = q.at[g, p, z]
        return remote(block, block, qz_s.at[g, k], qz_r.at[g, k], at_z(k, 1) * NP + p, t)

    def q_p(g, j):
        block = q.at[g, p]
        return remote(block, block, qp_s.at[g, j], qp_r.at[g, j], z * NP + plane(j, 1), t)

    for g in range(2):
        for k in range(1, NZ):
            q_z(g, k).start()

    leaf_length = lengths[z]
    pad = jnp.zeros((HD - 8, HD), F32)
    own_keys, own_values = sk_in[...].astype(F32), sv_in[...].astype(F32)
    for g in range(2):
        cols = slice(g * HD, (g + 1) * HD)
        sk[g] = jnp.concatenate([own_keys[:, cols], pad], axis=0).astype(BF16)
        sv[g] = jnp.concatenate([own_values[:, cols], pad], axis=0).astype(BF16)
    for leaf in range(NZ):
        current = jnp.int32(leaf)
        linked = jnp.int32(0)
        for _ in range(NZ):
            following = parents[current]
            hit = jnp.where(following != current, jnp.int32(1), jnp.int32(0))
            linked = jnp.maximum(linked, jnp.where(following == z, hit, jnp.int32(0)))
            current = following
        anc[leaf * LEAF_ROWS : (leaf + 1) * LEAF_ROWS, :] = jnp.full((LEAF_ROWS, HD), linked, jnp.int32)
    zeros = jnp.zeros((4 * HD, 64), BF16)
    for g in range(2):
        part = w_in[g * 4 * HD : (g + 1) * 4 * HD, :]
        w2[g, 0 : 4 * HD, :] = jnp.concatenate([part, zeros], axis=1)
        w2[g, 4 * HD : 8 * HD, :] = jnp.concatenate([zeros, part], axis=1)

    for g in range(2):
        for k in range(1, NZ):
            q_z(g, k).wait_recv()
        for j in range(1, NP):
            q_p(g, j).start()
    for load in loads:
        load.wait()

    row = lax.broadcasted_iota(jnp.int32, (ROWS, HD), 0)
    lane = lax.broadcasted_iota(jnp.int32, (ROWS, HD), 1)
    place = p * 8 + lane
    live = (lane < 8) & (place < leaf_length)
    same_leaf = (row // LEAF_ROWS) == z
    eye = lax.broadcasted_iota(jnp.int32, (HD, HD), 0) == lax.broadcasted_iota(jnp.int32, (HD, HD), 1)
    ones = jnp.ones((TILE, HD), BF16)

    def send_a(g, j):
        return remote(
            sums.at[g, j], recv_a.at[g, j], a_s.at[g, j], a_r.at[g, j], z * NP + plane(j, -1), t
        )

    def attend(g, first):
        blocks, masks = [], []
        for j in (first, first + 1):
            source = plane(j, -1)
            blocks.append(q[g, source].reshape(ROWS, HD))
            own_row = same_leaf & (place <= source * 8 + row % 8)
            masks.append(jnp.where(live & (own_row | (anc[...] > 0)), 1.0, 0.0))
        scaled = jnp.concatenate(blocks, axis=0).astype(F32) * SCALE
        hi = scaled.astype(BF16)
        low = (scaled - hi.astype(F32)).astype(BF16)
        query = jnp.concatenate([hi, low], axis=1)
        allowed = jnp.concatenate(masks, axis=0) > 0.5

        def scores(block):
            return lax.dot_general(
                query, jnp.concatenate([block, block], axis=1),
                (((1,), (1,)), ((), ())), preferred_element_type=F32,
            )

        leaf_scores = jnp.where(allowed, scores(sk[g]), LOW)
        following = scores(keys[g, 0:TILE, :])
        peak = jnp.max(leaf_scores, axis=1, keepdims=True)
        weight = jnp.where(allowed, jnp.exp2(leaf_scores - peak), 0.0).astype(BF16)
        total = jnp.dot(
            weight, jnp.concatenate([sv[g], ones[:HD]], axis=1), preferred_element_type=F32
        )
        for tile in range(KEYS // TILE):
            now = following
            raised = jnp.maximum(peak, jnp.max(now, axis=1, keepdims=True))
            if tile + 1 < KEYS // TILE:
                following = scores(keys[g, (tile + 1) * TILE : (tile + 2) * TILE, :])
            weight = jnp.exp2(now - raised).astype(BF16)
            table = jnp.concatenate([values[g, tile * TILE : (tile + 1) * TILE, :], ones], axis=1)
            total = total * jnp.exp2(peak - raised) + jnp.dot(weight, table, preferred_element_type=F32)
            peak = raised
        mean = (total[:, :HD] / total[:, HD:]).astype(BF16)
        lam = (peak + jnp.log2(total[:, HD:])).reshape(2, 2, HD, HD)
        lam = jnp.sum(jnp.where(eye[None, None], lam, 0.0), axis=2)
        for i in range(2):
            sums[g, first + i, 0:ROWS, :] = mean[i * ROWS : (i + 1) * ROWS]
            sums[g, first + i, ROWS : ROWS + TAIL, :] = pack_tail(lam[i])

    def send_b(g, k):
        return remote(
            part_b.at[g, at_z(k, 1)], recv_b.at[g, k], b_s.at[g, k], b_r.at[g, k], at_z(k, 1) * NP + p, t
        )

    def merge_plane(g):
        for j in range(1, NP):
            send_a(g, j).wait_recv()
        held = [sums.at[g, 0]] + [recv_a.at[g, j] for j in range(1, NP)]
        lams = [read_tail(block[ROWS : ROWS + TAIL, :]) for block in held]
        peak = lams[0]
        for lam in lams[1:]:
            peak = jnp.maximum(peak, lam)
        weights = [jnp.exp2(lam - peak) for lam in lams]
        whole = sum(weights[1:], weights[0])
        tail = pack_tail(peak + jnp.log2(whole))
        weights = [weight / whole for weight in weights]
        for half in range(2):
            merged = None
            for block, weight in zip(held, weights):
                column = jnp.sum(jnp.where(eye, weight[half : half + 1], 0.0), axis=1, keepdims=True)
                term = column * block[half * HD : (half + 1) * HD, :].astype(F32)
                merged = term if merged is None else merged + term
            merged = merged.astype(BF16)
            for i in range(4):
                part_b[g, 4 * half + i, 0:LEAF_ROWS, :] = merged[i * LEAF_ROWS : (i + 1) * LEAF_ROWS]
                part_b[g, 4 * half + i, LEAF_ROWS : LEAF_ROWS + TAIL, :] = tail
        for k in range(1, NZ):
            send_b(g, k).start()

    def att_z(g, k):
        block = att.at[g, p, z]
        return remote(block, block, gz_s.at[g, k], gz_r.at[g, k], at_z(k, 1) * NP + p, t)

    def att_p(g, j):
        block = att.at[g, p]
        return remote(block, block, gp_s.at[g, j], gp_r.at[g, j], z * NP + plane(j, 1), t)

    def merge_z(g):
        for k in range(1, NZ):
            send_b(g, k).wait_recv()
        shape = (LEAF_ROWS, HD)
        spot = lax.broadcasted_iota(jnp.int32, shape, 1) == (
            lax.broadcasted_iota(jnp.int32, shape, 0) + LEAF_ROWS * (z % 4)
        )
        held = [part_b[g, z]] + [recv_b[g, k] for k in range(1, NZ)]
        lams = []
        for block in held:
            lam = read_tail(block[LEAF_ROWS : LEAF_ROWS + TAIL])
            line = jnp.where(z // 4 == 0, lam[0:1], lam[1:2])
            lams.append(jnp.sum(jnp.where(spot, line, 0.0), axis=1, keepdims=True))
        peak = lams[0]
        for lam in lams[1:]:
            peak = jnp.maximum(peak, lam)
        top, whole = None, None
        for block, lam in zip(held, lams):
            weight = jnp.exp2(lam - peak)
            term = weight * block[:LEAF_ROWS].astype(F32)
            top = term if top is None else top + term
            whole = weight if whole is None else whole + weight
        att[g, p, z] = (top / whole).astype(BF16)
        for k in range(1, NZ):
            att_z(g, k).start()

    def spread_plane(g):
        for k in range(1, NZ):
            att_z(g, k).wait_recv()
        for j in range(1, NP):
            att_p(g, j).start()

    def project(g):
        for j in range(1, NP):
            att_p(g, j).wait_recv()
        lines = []
        for source in range(NP):
            rows = att[g, source].astype(F32).reshape(NT, 2, 4, 8, HD)
            parts = [rows[:, side, h].reshape(NT * 8, HD) for side in range(2) for h in range(4)]
            lines.append(jnp.concatenate(parts, axis=1))
        lines = jnp.concatenate(lines, axis=0).astype(BF16)
        return jnp.dot(lines, w2[g], preferred_element_type=F32).reshape(NP, NT, 8, HD)

    def step(i, carry):
        g, first = i // 4, (i % 4) * 2

        for j in (first, first + 1):

            @pl.when(j > 0)
            def _():
                q_p(g, j).wait_recv()

        @pl.when(i == 5)
        def _():
            merge_plane(0)

        @pl.when(i == 6)
        def _():
            merge_z(0)

        @pl.when(i == 7)
        def _():
            spread_plane(0)

        attend(g, first)
        for j in (first, first + 1):

            @pl.when(j > 0)
            def _():
                send_a(g, j).start()

        return carry

    lax.fori_loop(0, 8, step, 0)
    merge_plane(1)
    merge_z(1)
    spread_plane(1)
    projected = project(0)
    projected = projected + project(1)

    def share(k):
        to = (t + k) % NT
        return remote(proj.at[to], recv_p.at[k], t_s.at[k], t_r.at[k], c, to)

    for to in range(NT):
        proj[to] = projected[:, to]
    for k in range(1, NT):
        share(k).start()
    for k in range(1, NT):
        share(k).wait_recv()
    total = proj[t]
    for k in range(1, NT):
        total = total + recv_p[k]
    total = total.reshape(NP * 8, HD)
    out_ref[0:64, :] = (res_in[0:64, :].astype(F32) + total[:, :64]).astype(BF16)
    out_ref[64:128, :] = (res_in[64:128, :].astype(F32) + total[:, 64:]).astype(BF16)

    for g in range(2):
        for k in range(1, NZ):
            q_z(g, k).wait_send()
            send_b(g, k).wait_send()
            att_z(g, k).wait_send()
        for j in range(1, NP):
            q_p(g, j).wait_send()
            send_a(g, j).wait_send()
            att_p(g, j).wait_send()
    for k in range(1, NT):
        share(k).wait_send()


def shards(queries, suffix_keys, suffix_values, prefix_keys, prefix_values, lengths, parents, out_weight, residual):
    vmem, smem, hbm = (
        pl.BlockSpec(memory_space=pltpu.VMEM),
        pl.BlockSpec(memory_space=pltpu.SMEM),
        pl.BlockSpec(memory_space=pl.ANY),
    )
    dma = pltpu.SemaphoreType.DMA
    return pl.pallas_call(
        kernel,
        out_shape=jax.ShapeDtypeStruct(residual.shape, BF16),
        in_specs=[smem, smem, vmem, vmem, vmem, hbm, hbm, vmem, vmem],
        out_specs=vmem,
        scratch_shapes=[
            pltpu.VMEM((2, KEYS, HD), BF16),
            pltpu.VMEM((2, KEYS, HD), BF16),
            pltpu.VMEM((2, HD, HD), BF16),
            pltpu.VMEM((2, HD, HD), BF16),
            pltpu.VMEM((ROWS, HD), jnp.int32),
            pltpu.VMEM((2, 8 * HD, HD), BF16),
            pltpu.VMEM((2, NP, NZ, LEAF_ROWS, HD), BF16),
            pltpu.VMEM((2, NP, ROWS + TAIL, HD), BF16),
            pltpu.VMEM((2, NP, ROWS + TAIL, HD), BF16),
            pltpu.VMEM((2, NZ, LEAF_ROWS + TAIL, HD), BF16),
            pltpu.VMEM((2, NZ, LEAF_ROWS + TAIL, HD), BF16),
            pltpu.VMEM((2, NP, NZ, LEAF_ROWS, HD), BF16),
            pltpu.VMEM((NT, NP, 8, HD), F32),
            pltpu.VMEM((NT, NP, 8, HD), F32),
            dma((4,)),
            dma((2, NZ)), dma((2, NZ)),
            dma((2, NP)), dma((2, NP)),
            dma((2, NP)), dma((2, NP)),
            dma((2, NZ)), dma((2, NZ)),
            dma((2, NZ)), dma((2, NZ)),
            dma((2, NP)), dma((2, NP)),
            dma((NT,)), dma((NT,)),
        ],
        compiler_params=pltpu.CompilerParams(
            collective_id=0, has_side_effects=True, vmem_limit_bytes=48 << 20
        ),
        cost_estimate=pl.CostEstimate(
            flops=18 << 30, bytes_accessed=5 << 20, transcendentals=17 << 20
        ),
        name="cascade",
    )(lengths, parents, queries, suffix_keys, suffix_values, prefix_keys, prefix_values, out_weight, residual)


def solution(mesh):
    placed = (
        P("ctx", "tp"), P("ctx", "tp"), P("ctx", "tp"), P("ctx", "tp"), P("ctx", "tp"),
        P(), P(), P("tp", "ctx"), P("tp", "ctx"),
    )
    return jax.shard_map(shards, mesh=mesh, in_specs=placed, out_specs=P("tp", "ctx"), check_vma=False)
```

time: 1460 us -> 90.2 us (0.06)
  blocking collectives: 759 us -> 0 us
  waiting for transfers between devices: 488 us -> 0 us
  matrix products: 96.5 us -> 0 us
  Pallas kernels: 0 us -> 80.6 us
  other arithmetic: 48.1 us -> 0 us
  local copies, waits for them, and re-layouts: 47.8 us -> 9.18 us
    psum x1 -> x0, waiting for transfers between devices: 413 us -> none  [shards(): totals, weighted = lax.psum((totals, weighted), 'ctx')]
    all_gather x2 -> x0, blocking collectives: 260 us -> none  [the longest x1 135 us: shards(): lax.all_gather(suffix_values, 'ctx', axis=0, tiled=True)]
    psum x1 -> x0, blocking collectives: 249 us -> none  [shards(): totals, weighted = lax.psum((totals, weighted), 'ctx')]
    pmax x1 -> x0, blocking collectives: 249 us -> none  [shards(): highest = lax.pmax(block_peaks, 'ctx')]
    dot_general x20 -> x0, matrix products: 96.5 us -> none  [the longest x8 51.1 us: prefix_block(): jnp.einsum('bgrk,kgd->bgrd', weights, value_table, preferred_element_type...]
    pallas_call x0 -> x1, Pallas kernels: none -> 80.6 us  [shards(): pl.pallas_call(kernel, out_shape=jax.ShapeDtypeStruct(residual.shape, BF1...]
    reduce_scatter x1 -> x0, waiting for transfers between devices: 74.4 us -> none  [shards(): shares = lax.psum_scatter(projected, 'tp', scatter_dimension=0, tiled=True)]
    reduce_sum x17 -> x0, other arithmetic: 42.7 us -> none  [the longest x8 39 us: prefix_block(): block_total = jnp.sum(weights, axis=-1, dtype=jnp.float32)]
  transfers between devices with their start and end apart: 3 -> 0, of which waited for: 2 -> 0; matrix products, arithmetic and copies ran while one was open for 2% -> 0% of each run, Pallas kernels for 0% -> 0%
where the time goes in v1:
time: 90.2 us; the launch traced here: 89.8 us
  Pallas kernels  80.6 us (89%)
  local copies, waits for them, and re-layouts  9.18 us (10%)
    pallas_call x1, Pallas kernels, shards(): pl.pallas_call(kernel, out_shape=jax.ShapeDtypeStruct(residual.shape, BF1...  80.6 us
    unnamed x16, local copies, waits for them, and re-layouts  8.48 us

profile of v1, /device:TPU:1, one launch (start us, length us, event | category | flops | bytes accessed | tf_op | source)
XLA Modules:
  0.0 89.8 jit_solution(5466716117198466029)
XLA Ops:
  0.0 0.8 copy.11.res_in
  0.8 1.1 %copy.10.w_in = bf16[1024,64]{1,0:T(8,128)(2,1)S(1)} copy(bf16[1024,64]{0,1:T(8,128)(2,1)} %param.16) | data formatting | bytes 262144 | tf_op args[7]
  1.9 0.0 copy-start
  1.9 1.6 %copy-done = bf16[4096,256]{1,0:T(8,128)(2,1)S(1)} copy-done((bf16[4096,256]{1,0:T(8,128)(2,1)S(1)}, bf16[4096,256]{1,0:T(8,128)(2,1)}, u32[]{:S(2)}) %copy-start) | copy-done | bytes 2097176
  3.5 0.0 copy-start.1
  3.5 1.6 %copy-done.1 = bf16[4096,256]{1,0:T(8,128)(2,1)S(1)} copy-done((bf16[4096,256]{1,0:T(8,128)(2,1)S(1)}, bf16[4096,256]{1,0:T(8,128)(2,1)}, u32[]{:S(2)}) %copy-start.1) | copy-done | bytes 2097176
  5.1 0.0 copy-start.2
  5.1 0.7 copy-done.2
  5.8 0.0 copy-start.3
  5.8 0.7 copy-done.3
  6.5 0.0 copy-start.4
  6.5 0.7 copy-done.4
  7.2 0.0 copy-start.5
  7.2 0.7 copy-done.5
  7.9 0.0 copy-start.6
  7.9 0.7 copy-done.6
  8.5 80.6 %cascade.1 = bf16[128,64]{1,0:T(8,128)(2,1)S(1)} custom-call(s32[8]{0:T(128)S(1)} %copy-done.5, s32[8]{0:T(128)S(1)} %copy-done.6, bf16[8,1024]{1,0:T(8,128)(2,1)S(1)} %copy-done.2, bf16[8,256]{1,0:T(8,128)(2,1)S(1)} %copy-done.3, bf16[8,256]{1,0:T(8,128)(2,1)S(1)} %copy-done.4, bf16[4096,256]{1,0:T(8,128)(2,1)S(1)} %copy-done, ...), custom_call_target="tpu_custom_call" | custom-call | flops 19327352832 | bytes 5242880 | tf_op jit(solution)/shard_map/cascade/pallas_call | solution.py:340
  89.1 0.7 copy.12
Async XLA Ops:
  1.9 1.6 %copy-start = (bf16[4096,256]{1,0:T(8,128)(2,1)S(1)}, bf16[4096,256]{1,0:T(8,128)(2,1)}, u32[]{:S(2)}) copy-start(bf16[4096,256]{1,0:T(8,128)(2,1)} %pk_hbm.1) | copy-start | bytes 6291460
  3.5 1.6 %copy-start.1 = (bf16[4096,256]{1,0:T(8,128)(2,1)S(1)}, bf16[4096,256]{1,0:T(8,128)(2,1)}, u32[]{:S(2)}) copy-start(bf16[4096,256]{1,0:T(8,128)(2,1)} %pv_hbm.1) | copy-start | bytes 6291460
  5.1 0.7 copy-start.2
  5.8 0.7 copy-start.3
  6.5 0.7 copy-start.4
  7.2 0.7 copy-start.5
  7.9 0.7 copy-start.6

commit v2 on v1

v2 whole, which is shorter than its diff:
```python
import math

import jax
import jax.numpy as jnp
from jax import lax
from jax.experimental import pallas as pl
from jax.experimental.pallas import tpu as pltpu
from jax.sharding import PartitionSpec as P

HD = 128
NX, NY, NZ = 4, 2, 8
NP = NX * NY
NT = 4
LEAF_ROWS = 32
ROWS = NZ * LEAF_ROWS
TAIL = 16
KEYS = 4096
TILE = 1024
SCALE = math.log2(math.e) / math.sqrt(HD)
LOW = -1e30
F32, BF16 = jnp.float32, jnp.bfloat16
MESH = pl.DeviceIdType.MESH


def split3(x):
    hi = x.astype(BF16).astype(F32)
    rest = x - hi
    mid = rest.astype(BF16).astype(F32)
    low = (rest - mid).astype(BF16).astype(F32)
    return hi, mid, low


def pack_tail(lam):
    zeros = jnp.zeros((TAIL - 6, 128), F32)
    return jnp.concatenate([*split3(lam), zeros], axis=0).astype(BF16)


def read_tail(tail):
    tail = tail.astype(F32)
    return tail[0:2] + tail[2:4] + tail[4:6]


def kernel(
    lengths_in, parents_in, q_hbm, sk_hbm, sv_hbm, pk_hbm, pv_hbm, w_hbm, res_hbm, out_ref,
    lengths, parents, q_in, sk_in, sv_in, res_in, keys, values, weights, sk, sv, anc, q, sums, recv_y, recv_x, part_b, recv_b, att,
    shares_out, shares_in,
    load_sem, qz_s, qz_r, qx_s, qx_r, qh_s, qh_r, qy_s, qy_r, w_s, w_r, ay_s, ay_r, ax_s, ax_r, b_s, b_r, c_s, c_r, d_s, d_r,
):
    far_first = (4, 3, 5, 2, 6, 1, 7)
    c, t = lax.axis_index("ctx"), lax.axis_index("tp")
    z, p = c // NP, c % NP
    y, x = p // NX, p % NX

    def plane(j, sign):
        xx = (x + NX + sign * (j % NX)) % NX
        yy = (y + NY + sign * (j // NX)) % NY
        return yy * NX + xx

    def at_z(k, sign):
        return (z + NZ + sign * k) % NZ

    def remote(src, dst, send, recv, ctx, tp):
        return pltpu.make_async_remote_copy(
            src_ref=src, dst_ref=dst, send_sem=send, recv_sem=recv,
            device_id=(ctx, tp), device_id_type=MESH,
        )

    early = pltpu.make_async_copy(q_hbm, q_in, load_sem.at[4])
    early.start()
    loads = []
    for k, (src, dst) in enumerate(
        ((lengths_in, lengths), (parents_in, parents), (sk_hbm, sk_in), (sv_hbm, sv_in), (w_hbm, weights.at[z]), (res_hbm, res_in))
    ):
        loads.append(pltpu.make_async_copy(src, dst, load_sem.at[5 + k]))
    for g in range(2):
        cols = pl.ds(g * HD, HD)
        loads.append(pltpu.make_async_copy(pk_hbm.at[:, cols], keys.at[g], load_sem.at[2 * g]))
        loads.append(pltpu.make_async_copy(pv_hbm.at[:, cols], values.at[g], load_sem.at[2 * g + 1]))
    for load in loads:
        load.start()

    barrier = pltpu.get_barrier_semaphore()
    for k in (*far_first, 0):
        for i in range(NT):
            if k or i:
                there = (at_z(k, 1) * NP + p, (t + i) % NT)
                pl.semaphore_signal(barrier, inc=1, device_id=there, device_id_type=MESH)
    for j in range(1, NP):
        pl.semaphore_signal(barrier, inc=1, device_id=(z * NP + plane(j, 1), t), device_id_type=MESH)

    early.wait()
    own = q_in[...].astype(F32)
    for g in range(2):
        heads = [own[:, (4 * g + h) * HD : (4 * g + h + 1) * HD] for h in range(4)]
        q[g, p, z] = jnp.concatenate(heads, axis=0).astype(BF16)
    pl.semaphore_wait(barrier, NZ * NT - 1 + NP - 1)

    def q_z(g, k):
        block = q.at[g, p, z]
        return remote(block, block, qz_s.at[g, k], qz_r.at[g, k], at_z(k, 1) * NP + p, t)

    across = z * NP + (1 - y) * NX + x

    def q_x(g, j):
        block = q.at[g, plane(j - j % NX, -1)]
        return remote(block, block, qx_s.at[g, j], qx_r.at[g, j], z * NP + plane(j % NX, 1), t)

    def q_half(g, side):
        j = 1 + 2 * side
        block = q.at[g, plane(j, -1), pl.ds(side * 4, 4)]
        return remote(block, block, qh_s.at[g, side], qh_r.at[g, side], z * NP + plane(j, 1), t)

    def q_y(g, j):
        block = q.at[g, plane(j, -1)]
        return remote(block, block, qy_s.at[g, j], qy_r.at[g, j], across, t)

    def round_1(g):
        for k in far_first:
            q_z(g, k).wait_recv()
        q_x(g, 1).start()
        q_x(g, 3).start()
        q_y(g, 0).start()

    def round_2(g):
        for j in (1, 3):
            q_x(g, j).wait_recv()
        q_half(g, 0).start()
        q_half(g, 1).start()
        q_y(g, 0).wait_recv()
        q_x(g, 5).start()
        q_x(g, 7).start()

    def round_3(g):
        q_half(g, 0).wait_recv()
        q_half(g, 1).wait_recv()
        q_y(g, 2).start()

    def pass_w(hop, sign):
        block = weights.at[at_z(hop - 1, -sign)]
        side = (1 - sign) // 2
        return remote(block, block, w_s.at[side, hop], w_r.at[side, hop], at_z(1, sign) * NP + p, t)

    for k in far_first:
        q_z(0, k).start()

    for load in loads:
        load.wait()
    leaf_length = lengths[z]
    pad = jnp.zeros((HD - 8, HD), F32)
    own_keys, own_values = sk_in[...].astype(F32), sv_in[...].astype(F32)
    for g in range(2):
        cols = slice(g * HD, (g + 1) * HD)
        sk[g] = jnp.concatenate([own_keys[:, cols], pad], axis=0).astype(BF16)
        sv[g] = jnp.concatenate([own_values[:, cols], pad], axis=0).astype(BF16)
    for leaf in range(NZ):
        current = jnp.int32(leaf)
        linked = jnp.int32(0)
        for _ in range(NZ):
            following = parents[current]
            hit = jnp.where(following != current, jnp.int32(1), jnp.int32(0))
            linked = jnp.maximum(linked, jnp.where(following == z, hit, jnp.int32(0)))
            current = following
        anc[leaf * LEAF_ROWS : (leaf + 1) * LEAF_ROWS, :] = jnp.full((LEAF_ROWS, HD), linked, jnp.int32)
    round_1(0)
    for k in far_first:
        q_z(1, k).start()
    pass_w(1, 1).start()
    pass_w(1, -1).start()

    row = lax.broadcasted_iota(jnp.int32, (ROWS, HD), 0)
    lane = lax.broadcasted_iota(jnp.int32, (ROWS, HD), 1)
    place = p * 8 + lane
    live = (lane < 8) & (place < leaf_length)
    same_leaf = (row // LEAF_ROWS) == z
    eye = lax.broadcasted_iota(jnp.int32, (HD, HD), 0) == lax.broadcasted_iota(jnp.int32, (HD, HD), 1)
    ones = jnp.ones((TILE, HD), BF16)

    def send_y(g, j):
        return remote(sums.at[g, NX + j], recv_y.at[g, j], ay_s.at[g, j], ay_r.at[g, j], across, t)

    def send_x(g, j):
        return remote(sums.at[g, j], recv_x.at[g, j], ax_s.at[g, j], ax_r.at[g, j], z * NP + plane(j, -1), t)

    def attend(g, pair):
        blocks, masks = [], []
        for j in pair:
            source = plane(j, -1)
            blocks.append(q[g, source].reshape(ROWS, HD))
            own_row = same_leaf & (place <= source * 8 + row % 8)
            masks.append(jnp.where(live & (own_row | (anc[...] > 0)), 1.0, 0.0))
        scaled = jnp.concatenate(blocks, axis=0).astype(F32) * SCALE
        hi = scaled.astype(BF16)
        low = (scaled - hi.astype(F32)).astype(BF16)
        query = jnp.concatenate([hi, low], axis=1)
        allowed = jnp.concatenate(masks, axis=0) > 0.5

        def scores(block):
            return lax.dot_general(
                query, jnp.concatenate([block, block], axis=1),
                (((1,), (1,)), ((), ())), preferred_element_type=F32,
            )

        leaf_scores = jnp.where(allowed, scores(sk[g]), LOW)
        following = scores(keys[g, 0:TILE, :])
        peak = jnp.max(leaf_scores, axis=1, keepdims=True)
        weight = jnp.where(allowed, jnp.exp2(leaf_scores - peak), 0.0).astype(BF16)
        total = jnp.dot(
            weight, jnp.concatenate([sv[g], ones[:HD]], axis=1), preferred_element_type=F32
        )
        for tile in range(KEYS // TILE):
            now = following
            raised = jnp.maximum(peak, jnp.max(now, axis=1, keepdims=True))
            if tile + 1 < KEYS // TILE:
                following = scores(keys[g, (tile + 1) * TILE : (tile + 2) * TILE, :])
            weight = jnp.exp2(now - raised).astype(BF16)
            table = jnp.concatenate([values[g, tile * TILE : (tile + 1) * TILE, :], ones], axis=1)
            total = total * jnp.exp2(peak - raised) + jnp.dot(weight, table, preferred_element_type=F32)
            peak = raised
        mean = (total[:, :HD] / total[:, HD:]).astype(BF16)
        lam = (peak + jnp.log2(total[:, HD:])).reshape(2, 2, HD, HD)
        lam = jnp.sum(jnp.where(eye[None, None], lam, 0.0), axis=2)
        for i, j in enumerate(pair):
            sums[g, j, 0:ROWS, :] = mean[i * ROWS : (i + 1) * ROWS]
            sums[g, j, ROWS : ROWS + TAIL, :] = pack_tail(lam[i])

    def send_b(g, k):
        return remote(
            part_b.at[g, at_z(k, 1)], recv_b.at[g, k], b_s.at[g, k], b_r.at[g, k], at_z(k, 1) * NP + p, t
        )

    def merge_pair(g, j):
        send_y(g, j).wait_recv()
        ours, theirs = sums.at[g, j], recv_y.at[g, j]
        lam_a, lam_b = read_tail(ours[ROWS : ROWS + TAIL, :]), read_tail(theirs[ROWS : ROWS + TAIL, :])
        peak = jnp.maximum(lam_a, lam_b)
        whole = peak + jnp.log2(jnp.exp2(lam_a - peak) + jnp.exp2(lam_b - peak))
        weight = jnp.exp2(lam_a - whole)
        for half in range(2):
            span = slice(half * HD, (half + 1) * HD)
            column = jnp.sum(jnp.where(eye, weight[half : half + 1], 0.0), axis=1, keepdims=True)
            a, b = ours[span, :].astype(F32), theirs[span, :].astype(F32)
            ours[span, :] = (b + column * (a - b)).astype(BF16)
        ours[ROWS : ROWS + TAIL, :] = pack_tail(whole)
        if j:
            send_x(g, j).start()

    def merge_plane(g):
        for j in range(1, NX):
            send_x(g, j).wait_recv()
        held = [sums.at[g, 0]] + [recv_x.at[g, j] for j in range(1, NX)]
        lams = [read_tail(block[ROWS : ROWS + TAIL, :]) for block in held]
        peak = lams[0]
        for lam in lams[1:]:
            peak = jnp.maximum(peak, lam)
        weights = [jnp.exp2(lam - peak) for lam in lams]
        whole = sum(weights[1:], weights[0])
        tail = pack_tail(peak + jnp.log2(whole))
        weights = [weight / whole for weight in weights]
        for half in range(2):
            merged = None
            for block, weight in zip(held, weights):
                column = jnp.sum(jnp.where(eye, weight[half : half + 1], 0.0), axis=1, keepdims=True)
                term = column * block[half * HD : (half + 1) * HD, :].astype(F32)
                merged = term if merged is None else merged + term
            merged = merged.astype(BF16)
            for i in range(4):
                part_b[g, 4 * half + i, 0:LEAF_ROWS, :] = merged[i * LEAF_ROWS : (i + 1) * LEAF_ROWS]
                part_b[g, 4 * half + i, LEAF_ROWS : LEAF_ROWS + TAIL, :] = tail
        for k in far_first:
            send_b(g, k).start()

    def att_p(g, j):
        block = att.at[g, p]
        return remote(block, block, c_s.at[g, j], c_r.at[g, j], z * NP + plane(j, 1), t)

    def merge_z(g):
        for k in range(1, NZ):
            send_b(g, k).wait_recv()
        shape = (LEAF_ROWS, HD)
        spot = lax.broadcasted_iota(jnp.int32, shape, 1) == (
            lax.broadcasted_iota(jnp.int32, shape, 0) + LEAF_ROWS * (z % 4)
        )
        held = [part_b[g, z]] + [recv_b[g, k] for k in range(1, NZ)]
        lams = []
        for block in held:
            lam = read_tail(block[LEAF_ROWS : LEAF_ROWS + TAIL])
            line = jnp.where(z // 4 == 0, lam[0:1], lam[1:2])
            lams.append(jnp.sum(jnp.where(spot, line, 0.0), axis=1, keepdims=True))
        peak = lams[0]
        for lam in lams[1:]:
            peak = jnp.maximum(peak, lam)
        top, whole = None, None
        for block, lam in zip(held, lams):
            weight = jnp.exp2(lam - peak)
            term = weight * block[:LEAF_ROWS].astype(F32)
            top = term if top is None else top + term
            whole = weight if whole is None else whole + weight
        att[g, p] = (top / whole).astype(BF16)
        for j in (6, 5, 7, 2, 4, 1, 3):
            att_p(g, j).start()

    def project(g):
        for j in range(1, NP):
            att_p(g, j).wait_recv()
        rows = [att[g, source].astype(F32) for source in range(NP)]
        heads = []
        for h in range(4):
            heads.append(jnp.concatenate([block[8 * h : 8 * h + 8] for block in rows], axis=0))
        tokens = jnp.concatenate(heads, axis=1).astype(BF16)
        table = weights[:, :, g * 4 * HD : (g + 1) * 4 * HD].reshape(NZ * 64, 4 * HD)
        return lax.dot_general(table, tokens, (((1,), (1,)), ((), ())), preferred_element_type=F32)

    def step(i, carry):
        g, k = i // 4, i % 4

        def of_step(table):
            values = []
            for a, b, c, d in table:
                second, third = c - 2 * b + a, d - 3 * c + 3 * b - a
                value = a + (b - a) * k + second * (k * (k - 1) // 2) + third * (k * (k - 1) * (k - 2) // 6)
                values.append(value)
            return values[0] * (1 - g) + values[1] * g

        pair = (of_step(((0, 3, 5, 2), (5, 1, 2, 0))), of_step(((1, 4, 7, 6), (7, 6, 3, 4))))

        @pl.when(i == 0)
        def _():
            round_2(0)
            round_1(1)

        @pl.when(i == 1)
        def _():
            round_3(0)

        @pl.when(i == 2)
        def _():
            round_2(1)
            q_x(0, 5).wait_recv()
            q_x(0, 7).wait_recv()

        @pl.when(i == 3)
        def _():
            q_y(0, 2).wait_recv()
            round_3(1)

        @pl.when(i == 4)
        def _():
            q_x(1, 5).wait_recv()
            q_x(1, 7).wait_recv()

        @pl.when(i == 5)
        def _():
            q_y(1, 2).wait_recv()

        for hop in (2, 3, 4):

            @pl.when(i == 2 * hop - 2)
            def _():
                pass_w(hop - 1, 1).wait_recv()
                pass_w(hop, 1).start()
                pass_w(hop - 1, -1).wait_recv()
                if hop < 4:
                    pass_w(hop, -1).start()

        @pl.when(i == 6)
        def _():
            for j in (2, 1, 3, 0):
                merge_pair(0, j)

        @pl.when(i == 7)
        def _():
            merge_pair(1, 1)
            merge_pair(1, 3)
            merge_pair(1, 2)

        attend(g, pair)
        for j in pair:

            @pl.when(j >= NX)
            def _():
                send_y(g, j - NX).start()

        return carry

    lax.fori_loop(0, 8, step, 0)
    merge_plane(0)
    merge_pair(1, 0)
    merge_plane(1)
    merge_z(0)
    merge_z(1)
    pass_w(4, 1).wait_recv()
    projected = project(0)
    projected = projected + project(1)
    for k in range(NZ):
        block = projected[64 * k : 64 * k + 64]
        shares_out[k] = jnp.concatenate([block[:32], block[32:]], axis=1).astype(BF16)

    home = z // 2
    slot = (z % 2) * NT + t

    def share(k):
        to = at_z(k, 1)
        return remote(shares_out.at[to], shares_in.at[slot], d_s.at[k], d_r.at[slot], to * NP + p, home)

    stays = home == t
    for k in far_first:
        share(k).start()

    @pl.when(jnp.logical_not(stays))
    def _():
        share(0).start()

    @pl.when(stays)
    def _():
        shares_in[slot] = shares_out[z]

    for side in range(2):
        for i in range(NT):

            @pl.when(jnp.logical_not((2 * t + side == z) & (t == i)))
            def _():
                here = shares_in.at[side * NT + i]
                remote(here, here, d_s.at[0], d_r.at[side * NT + i], (2 * t + side) * NP + p, i).wait_recv()

    sides = []
    for side in range(2):
        parts = [shares_in[side * NT + i].astype(F32) for i in range(NT)]
        sides.append((parts[0] + parts[1]) + (parts[2] + parts[3]))
    top = jnp.concatenate([sides[0][:, :64], sides[1][:, :64]], axis=1)
    bottom = jnp.concatenate([sides[0][:, 64:], sides[1][:, 64:]], axis=1)
    out_ref[0:32, :] = (res_in[0:32, :].astype(F32) + top).astype(BF16)
    out_ref[32:64, :] = (res_in[32:64, :].astype(F32) + bottom).astype(BF16)

    for g in range(2):
        for k in range(1, NZ):
            q_z(g, k).wait_send()
            send_b(g, k).wait_send()
        for j in range(1, NP):
            att_p(g, j).wait_send()
        for j in (1, 3, 5, 7):
            q_x(g, j).wait_send()
        for side in range(2):
            q_half(g, side).wait_send()
            q_y(g, 2 * side).wait_send()
        for j in range(NX):
            send_y(g, j).wait_send()
        for j in range(1, NX):
            send_x(g, j).wait_send()
    for hop in range(1, 5):
        pass_w(hop, 1).wait_send()
        if hop < 4:
            pass_w(hop, -1).wait_send()
    for k in range(1, NZ):
        share(k).wait_send()

    @pl.when(jnp.logical_not(stays))
    def _():
        share(0).wait_send()


def shards(queries, suffix_keys, suffix_values, prefix_keys, prefix_values, lengths, parents, out_weight, residual):
    hbm = pl.BlockSpec(memory_space=pltpu.HBM)
    dma = pltpu.SemaphoreType.DMA
    flipped = pl.pallas_call(
        kernel,
        out_shape=jax.ShapeDtypeStruct(residual.shape[::-1], BF16),
        in_specs=[hbm] * 9,
        out_specs=pl.BlockSpec(memory_space=pltpu.VMEM),
        scratch_shapes=[
            pltpu.SMEM((8,), jnp.int32),
            pltpu.SMEM((8,), jnp.int32),
            pltpu.VMEM((8, 8 * HD), BF16),
            pltpu.VMEM((8, 2 * HD), BF16),
            pltpu.VMEM((8, 2 * HD), BF16),
            pltpu.VMEM((64, HD), BF16),
            pltpu.VMEM((2, KEYS, HD), BF16),
            pltpu.VMEM((2, KEYS, HD), BF16),
            pltpu.VMEM((NZ, 64, 8 * HD), BF16),
            pltpu.VMEM((2, HD, HD), BF16),
            pltpu.VMEM((2, HD, HD), BF16),
            pltpu.VMEM((ROWS, HD), jnp.int32),
            pltpu.VMEM((2, NP, NZ, LEAF_ROWS, HD), BF16),
            pltpu.VMEM((2, NP, ROWS + TAIL, HD), BF16),
            pltpu.VMEM((2, NX, ROWS + TAIL, HD), BF16),
            pltpu.VMEM((2, NX, ROWS + TAIL, HD), BF16),
            pltpu.VMEM((2, NZ, LEAF_ROWS + TAIL, HD), BF16),
            pltpu.VMEM((2, NZ, LEAF_ROWS + TAIL, HD), BF16),
            pltpu.VMEM((2, NP, LEAF_ROWS, HD), BF16),
            pltpu.VMEM((NZ, 32, HD), BF16),
            pltpu.VMEM((2 * NT, 32, HD), BF16),
            dma((11,)),
            dma((2, NZ)), dma((2, NZ)),
            dma((2, NP)), dma((2, NP)),
            dma((2, 2)), dma((2, 2)),
            dma((2, NX)), dma((2, NX)),
            dma((2, 5)), dma((2, 5)),
            dma((2, NX)), dma((2, NX)),
            dma((2, NX)), dma((2, NX)),
            dma((2, NZ)), dma((2, NZ)),
            dma((2, NP)), dma((2, NP)),
            dma((NZ,)), dma((2 * NT,)),
        ],
        compiler_params=pltpu.CompilerParams(
            collective_id=0, has_side_effects=True, vmem_limit_bytes=(64 << 20) - (64 << 10)
        ),
        cost_estimate=pl.CostEstimate(
            flops=18 << 30, bytes_accessed=5 << 20, transcendentals=17 << 20
        ),
        name="cascade",
    )(lengths, parents, queries, suffix_keys, suffix_values, prefix_keys, prefix_values, out_weight.T, residual.T)
    return flipped.T


def solution(mesh):
    placed = (
        P("ctx", "tp"), P("ctx", "tp"), P("ctx", "tp"), P("ctx", "tp"), P("ctx", "tp"),
        P(), P(), P("tp", "ctx"), P("tp", "ctx"),
    )
    return jax.shard_map(shards, mesh=mesh, in_specs=placed, out_specs=P("tp", "ctx"), check_vma=False)
```

time: 90.2 us -> 68 us (0.75)
  Pallas kernels: 80.6 us -> 66.4 us
  local copies, waits for them, and re-layouts: 9.18 us -> 1.32 us
    pallas_call x1, Pallas kernels: 80.6 us -> 66.4 us  [shards(): pl.pallas_call(kernel, out_shape=jax.ShapeDtypeStruct(residual.shape[::-1...]
    unnamed x16 -> x1, local copies, waits for them, and re-layouts: 8.48 us -> 1.32 us
where the time goes in v2:
time: 68 us; the launch traced here: 67.8 us
  Pallas kernels  66.4 us (98%)
  local copies, waits for them, and re-layouts  1.32 us (2%)
    pallas_call x1, Pallas kernels, shards(): pl.pallas_call(kernel, out_shape=jax.ShapeDtypeStruct(residual.shape[::-1...  66.4 us

profile of v2, /device:TPU:1, one launch (start us, length us, event | category | flops | bytes accessed | tf_op | source)
XLA Modules:
  0.0 67.8 jit_solution(2505108652465872821)
XLA Ops:
  0.0 66.4 %cascade.1 = bf16[64,128]{1,0:T(8,128)(2,1)} custom-call(s32[8]{0:T(128)} %lengths_in.1, s32[8]{0:T(128)} %parents_in.1, bf16[8,1024]{1,0:T(8,128)(2,1)} %q_hbm.1, bf16[8,256]{1,0:T(8,128)(2,1)} %sk_hbm.1, bf16[8,256]{1,0:T(8,128)(2,1)} %sv_hbm.1, bf16[4096,256]{1,0:T(8,128)(2,1)} %pk_hbm.1, bf16[4096,256]{1,0:T(8,128)(2,1)} %pv_hbm.1, ...), custom_call_target="tpu_custom_call" | custom-call | flops 19327352832 | bytes 5242880 | tf_op jit(solution)/shard_map/cascade/pallas_call | solution.py:464
  66.4 1.3 %copy.11 = bf16[128,64]{0,1:T(8,128)(2,1)} copy(bf16[128,64]{0,1:T(8,128)(2,1)} %bitcast.3) | data formatting | bytes 32768

commit v3 on v2

--- a/solution.py
+++ b/solution.py
@@ -67,6 +67,16 @@
 
     early = pltpu.make_async_copy(q_hbm, q_in, load_sem.at[4])
     early.start()
+    barrier = pltpu.get_barrier_semaphore()
+    for k in far_first:
+        pl.semaphore_signal(barrier, inc=1, device_id=(at_z(k, 1) * NP + p, t), device_id_type=MESH)
+    for j in range(1, NP):
+        pl.semaphore_signal(barrier, inc=1, device_id=(z * NP + plane(j, 1), t), device_id_type=MESH)
+    for side in range(2):
+        for i in range(1, NT):
+            there = ((2 * t + side) * NP + p, (t + i) % NT)
+            pl.semaphore_signal(barrier, inc=1, device_id=there, device_id_type=MESH)
+
     loads = []
     for k, (src, dst) in enumerate(
         ((lengths_in, lengths), (parents_in, parents), (sk_hbm, sk_in), (sv_hbm, sv_in), (w_hbm, weights.at[z]), (res_hbm, res_in))
@@ -79,51 +89,53 @@
     for load in loads:
         load.start()
 
-    barrier = pltpu.get_barrier_semaphore()
-    for k in (*far_first, 0):
-        for i in range(NT):
-            if k or i:
-                there = (at_z(k, 1) * NP + p, (t + i) % NT)
-                pl.semaphore_signal(barrier, inc=1, device_id=there, device_id_type=MESH)
-    for j in range(1, NP):
-        pl.semaphore_signal(barrier, inc=1, device_id=(z * NP + plane(j, 1), t), device_id_type=MESH)
-
     early.wait()
     own = q_in[...].astype(F32)
     for g in range(2):
         heads = [own[:, (4 * g + h) * HD : (4 * g + h + 1) * HD] for h in range(4)]
         q[g, p, z] = jnp.concatenate(heads, axis=0).astype(BF16)
-    pl.semaphore_wait(barrier, NZ * NT - 1 + NP - 1)
+    home = z // 2
+    stays = home == t
+
+    @pl.when(stays)
+    def _():
+        pl.semaphore_wait(barrier, NZ - 1 + NP - 1)
+
+    @pl.when(jnp.logical_not(stays))
+    def _():
+        pl.semaphore_wait(barrier, NZ - 1 + NP - 1 + NZ)
+
 
     def q_z(g, k):
         block = q.at[g, p, z]
-        return remote(block, block, qz_s.at[g, k], qz_r.at[g, k], at_z(k, 1) * NP + p, t)
+        return remote(block, block, qz_s.at[g], qz_r.at[g], at_z(k, 1) * NP + p, t)
 
     across = z * NP + (1 - y) * NX + x
+
+    def wait_all(ref, sem):
+        pltpu.make_async_copy(ref, ref, sem).wait()
 
     def q_x(g, j):
         block = q.at[g, plane(j - j % NX, -1)]
-        return remote(block, block, qx_s.at[g, j], qx_r.at[g, j], z * NP + plane(j % NX, 1), t)
+        return remote(block, block, qx_s.at[g], qx_r.at[g, j // NX], z * NP + plane(j % NX, 1), t)
 
     def q_half(g, side):
         j = 1 + 2 * side
         block = q.at[g, plane(j, -1), pl.ds(side * 4, 4)]
-        return remote(block, block, qh_s.at[g, side], qh_r.at[g, side], z * NP + plane(j, 1), t)
+        return remote(block, block, qh_s.at[g], qh_r.at[g], z * NP + plane(j, 1), t)
 
     def q_y(g, j):
         block = q.at[g, plane(j, -1)]
-        return remote(block, block, qy_s.at[g, j], qy_r.at[g, j], across, t)
+        return remote(block, block, qy_s.at[g], qy_r.at[g, j // 2], across, t)
 
     def round_1(g):
-        for k in far_first:
-            q_z(g, k).wait_recv()
+        wait_all(q.at[g, 0, pl.ds(0, NZ - 1)], qz_r.at[g])
         q_x(g, 1).start()
         q_x(g, 3).start()
         q_y(g, 0).start()
 
     def round_2(g):
-        for j in (1, 3):
-            q_x(g, j).wait_recv()
+        wait_all(q.at[g, pl.ds(0, 2)], qx_r.at[g, 0])
         q_half(g, 0).start()
         q_half(g, 1).start()
         q_y(g, 0).wait_recv()
@@ -131,14 +143,13 @@
         q_x(g, 7).start()
 
     def round_3(g):
-        q_half(g, 0).wait_recv()
-        q_half(g, 1).wait_recv()
+        wait_all(q.at[g, 0], qh_r.at[g])
         q_y(g, 2).start()
 
     def pass_w(hop, sign):
         block = weights.at[at_z(hop - 1, -sign)]
         side = (1 - sign) // 2
-        return remote(block, block, w_s.at[side, hop], w_r.at[side, hop], at_z(1, sign) * NP + p, t)
+        return remote(block, block, w_s.at[0], w_r.at[side, hop - 1], at_z(1, sign) * NP + p, t)
 
     for k in far_first:
         q_z(0, k).start()
@@ -176,14 +187,14 @@
     ones = jnp.ones((TILE, HD), BF16)
 
     def send_y(g, j):
-        return remote(sums.at[g, NX + j], recv_y.at[g, j], ay_s.at[g, j], ay_r.at[g, j], across, t)
+        return remote(sums.at[g, NX + j], recv_y.at[g, j], ay_s.at[g], ay_r.at[g, j], across, t)
 
     def send_x(g, j):
-        return remote(sums.at[g, j], recv_x.at[g, j], ax_s.at[g, j], ax_r.at[g, j], z * NP + plane(j, -1), t)
-
-    def attend(g, pair):
+        return remote(sums.at[g, j], recv_x.at[g, j], ax_s.at[g], ax_r.at[g], z * NP + plane(j, -1), t)
+
+    def attend(g, group):
         blocks, masks = [], []
-        for j in pair:
+        for j in group:
             source = plane(j, -1)
             blocks.append(q[g, source].reshape(ROWS, HD))
             own_row = same_leaf & (place <= source * 8 + row % 8)
@@ -217,15 +228,15 @@
             total = total * jnp.exp2(peak - raised) + jnp.dot(weight, table, preferred_element_type=F32)
             peak = raised
         mean = (total[:, :HD] / total[:, HD:]).astype(BF16)
-        lam = (peak + jnp.log2(total[:, HD:])).reshape(2, 2, HD, HD)
+        lam = (peak + jnp.log2(total[:, HD:])).reshape(len(group), 2, HD, HD)
         lam = jnp.sum(jnp.where(eye[None, None], lam, 0.0), axis=2)
-        for i, j in enumerate(pair):
+        for i, j in enumerate(group):
             sums[g, j, 0:ROWS, :] = mean[i * ROWS : (i + 1) * ROWS]
             sums[g, j, ROWS : ROWS + TAIL, :] = pack_tail(lam[i])
 
     def send_b(g, k):
         return remote(
-            part_b.at[g, at_z(k, 1)], recv_b.at[g, k], b_s.at[g, k], b_r.at[g, k], at_z(k, 1) * NP + p, t
+            part_b.at[g, at_z(k, 1)], recv_b.at[g, k], b_s.at[g], b_r.at[g], at_z(k, 1) * NP + p, t
         )
 
     def merge_pair(g, j):
@@ -245,8 +256,7 @@
             send_x(g, j).start()
 
     def merge_plane(g):
-        for j in range(1, NX):
-            send_x(g, j).wait_recv()
+        wait_all(recv_x.at[g, pl.ds(1, NX - 1)], ax_r.at[g])
         held = [sums.at[g, 0]] + [recv_x.at[g, j] for j in range(1, NX)]
         lams = [read_tail(block[ROWS : ROWS + TAIL, :]) for block in held]
         peak = lams[0]
@@ -271,11 +281,10 @@
 
     def att_p(g, j):
         block = att.at[g, p]
-        return remote(block, block, c_s.at[g, j], c_r.at[g, j], z * NP + plane(j, 1), t)
+        return remote(block, block, c_s.at[g], c_r.at[g], z * NP + plane(j, 1), t)
 
     def merge_z(g):
-        for k in range(1, NZ):
-            send_b(g, k).wait_recv()
+        wait_all(recv_b.at[g, pl.ds(1, NZ - 1)], b_r.at[g])
         shape = (LEAF_ROWS, HD)
         spot = lax.broadcasted_iota(jnp.int32, shape, 1) == (
             lax.broadcasted_iota(jnp.int32, shape, 0) + LEAF_ROWS * (z % 4)
@@ -300,8 +309,7 @@
             att_p(g, j).start()
 
     def project(g):
-        for j in range(1, NP):
-            att_p(g, j).wait_recv()
+        wait_all(att.at[g, pl.ds(0, NP - 1)], c_r.at[g])
         rows = [att[g, source].astype(F32) for source in range(NP)]
         heads = []
         for h in range(4):
@@ -311,50 +319,44 @@
         return lax.dot_general(table, tokens, (((1,), (1,)), ((), ())), preferred_element_type=F32)
 
     def step(i, carry):
-        g, k = i // 4, i % 4
-
         def of_step(table):
-            values = []
-            for a, b, c, d in table:
-                second, third = c - 2 * b + a, d - 3 * c + 3 * b - a
-                value = a + (b - a) * k + second * (k * (k - 1) // 2) + third * (k * (k - 1) * (k - 2) // 6)
-                values.append(value)
-            return values[0] * (1 - g) + values[1] * g
-
-        pair = (of_step(((0, 3, 5, 2), (5, 1, 2, 0))), of_step(((1, 4, 7, 6), (7, 6, 3, 4))))
-
-        @pl.when(i == 0)
+            return sum(entry * (1 // (1 + (i - s) * (i - s))) for s, entry in enumerate(table) if entry)
+
+        g = i // 5
+        first = of_step((0, 1, 4, 5, 2, 5, 6, 3, 4, 0))
+        second = of_step((0, 3, 0, 7, 6, 7, 1, 2, 0, 0))
+        single = (i == 0) | (i == 2) | (i >= 8)
+
+        @pl.when(i == 1)
         def _():
             round_2(0)
             round_1(1)
 
-        @pl.when(i == 1)
+        @pl.when(i == 2)
         def _():
             round_3(0)
 
-        @pl.when(i == 2)
+        @pl.when(i == 3)
         def _():
             round_2(1)
-            q_x(0, 5).wait_recv()
-            q_x(0, 7).wait_recv()
-
-        @pl.when(i == 3)
+            wait_all(q.at[0, pl.ds(0, 2)], qx_r.at[0, 1])
+
+        @pl.when(i == 4)
         def _():
             q_y(0, 2).wait_recv()
             round_3(1)
 
-        @pl.when(i == 4)
-        def _():
-            q_x(1, 5).wait_recv()
-            q_x(1, 7).wait_recv()
-
         @pl.when(i == 5)
         def _():
+            wait_all(q.at[1, pl.ds(0, 2)], qx_r.at[1, 1])
+
+        @pl.when(i == 6)
+        def _():
             q_y(1, 2).wait_recv()
 
         for hop in (2, 3, 4):
 
-            @pl.when(i == 2 * hop - 2)
+            @pl.when(i == 2 * hop - 1)
             def _():
                 pass_w(hop - 1, 1).wait_recv()
                 pass_w(hop, 1).start()
@@ -362,27 +364,36 @@
                 if hop < 4:
                     pass_w(hop, -1).start()
 
-        @pl.when(i == 6)
+        @pl.when(i == 7)
         def _():
             for j in (2, 1, 3, 0):
                 merge_pair(0, j)
 
-        @pl.when(i == 7)
+        @pl.when(i == 8)
         def _():
             merge_pair(1, 1)
             merge_pair(1, 3)
             merge_pair(1, 2)
 
-        attend(g, pair)
-        for j in pair:
-
-            @pl.when(j >= NX)
+        @pl.when(single)
+        def _():
+            attend(g, (first,))
+
+        @pl.when(jnp.logical_not(single))
+        def _():
+            attend(g, (first, second))
+
+            @pl.when(second >= NX)
             def _():
-                send_y(g, j - NX).start()
+                send_y(g, second - NX).start()
+
+        @pl.when(first >= NX)
+        def _():
+            send_y(g, first - NX).start()
 
         return carry
 
-    lax.fori_loop(0, 8, step, 0)
+    lax.fori_loop(0, 10, step, 0)
     merge_plane(0)
     merge_pair(1, 0)
     merge_plane(1)
@@ -395,14 +406,12 @@
         block = projected[64 * k : 64 * k + 64]
         shares_out[k] = jnp.concatenate([block[:32], block[32:]], axis=1).astype(BF16)
 
-    home = z // 2
     slot = (z % 2) * NT + t
 
     def share(k):
         to = at_z(k, 1)
-        return remote(shares_out.at[to], shares_in.at[slot], d_s.at[k], d_r.at[slot], to * NP + p, home)
-
-    stays = home == t
+        return remote(shares_out.at[to], shares_in.at[slot], d_s.at[1 // (k + 1)], d_r.at[slot], to * NP + p, home)
+
     for k in far_first:
         share(k).start()
 
@@ -432,26 +441,16 @@
     out_ref[32:64, :] = (res_in[32:64, :].astype(F32) + bottom).astype(BF16)
 
     for g in range(2):
-        for k in range(1, NZ):
-            q_z(g, k).wait_send()
-            send_b(g, k).wait_send()
-        for j in range(1, NP):
-            att_p(g, j).wait_send()
-        for j in (1, 3, 5, 7):
-            q_x(g, j).wait_send()
-        for side in range(2):
-            q_half(g, side).wait_send()
-            q_y(g, 2 * side).wait_send()
-        for j in range(NX):
-            send_y(g, j).wait_send()
-        for j in range(1, NX):
-            send_x(g, j).wait_send()
-    for hop in range(1, 5):
-        pass_w(hop, 1).wait_send()
-        if hop < 4:
-            pass_w(hop, -1).wait_send()
-    for k in range(1, NZ):
-        share(k).wait_send()
+        wait_all(q.at[g, 0, pl.ds(0, NZ - 1)], qz_s.at[g])
+        wait_all(q.at[g, pl.ds(0, 4)], qx_s.at[g])
+        wait_all(q.at[g, 0], qh_s.at[g])
+        wait_all(q.at[g, pl.ds(0, 2)], qy_s.at[g])
+        wait_all(sums.at[g, pl.ds(0, NX)], ay_s.at[g])
+        wait_all(sums.at[g, pl.ds(0, NX - 1)], ax_s.at[g])
+        wait_all(part_b.at[g, pl.ds(0, NZ - 1)], b_s.at[g])
+        wait_all(att.at[g, pl.ds(0, NP - 1)], c_s.at[g])
+    wait_all(weights.at[pl.ds(0, NZ - 1)], w_s.at[0])
+    wait_all(shares_out.at[pl.ds(0, NZ - 1)], d_s.at[0])
 
     @pl.when(jnp.logical_not(stays))
     def _():
@@ -489,16 +488,16 @@
             pltpu.VMEM((NZ, 32, HD), BF16),
             pltpu.VMEM((2 * NT, 32, HD), BF16),
             dma((11,)),
-            dma((2, NZ)), dma((2, NZ)),
-            dma((2, NP)), dma((2, NP)),
-            dma((2, 2)), dma((2, 2)),
-            dma((2, NX)), dma((2, NX)),
-            dma((2, 5)), dma((2, 5)),
-            dma((2, NX)), dma((2, NX)),
-            dma((2, NX)), dma((2, NX)),
-            dma((2, NZ)), dma((2, NZ)),
-            dma((2, NP)), dma((2, NP)),
-            dma((NZ,)), dma((2 * NT,)),
+            dma((2,)), dma((2,)),
+            dma((2,)), dma((2, 2)),
+            dma((2,)), dma((2,)),
+            dma((2,)), dma((2, 2)),
+            dma((1,)), dma((2, 4)),
+            dma((2,)), dma((2, NX)),
+            dma((2,)), dma((2,)),
+            dma((2,)), dma((2,)),
+            dma((2,)), dma((2,)),
+            dma((2,)), dma((2 * NT,)),
         ],
         compiler_params=pltpu.CompilerParams(
             collective_id=0, has_side_effects=True, vmem_limit_bytes=(64 << 20) - (64 << 10)

time: 68 us -> 64 us (0.941)
  Pallas kernels: 66.4 us -> 62.4 us
    pallas_call x1, Pallas kernels: 66.4 us -> 62.4 us  [shards(): pl.pallas_call(kernel, out_shape=jax.ShapeDtypeStruct(residual.shape[::-1...]
where the time goes in v3:
time: 64 us; the launch traced here: 63.8 us
  Pallas kernels  62.4 us (98%)
  local copies, waits for them, and re-layouts  1.32 us (2%)
    pallas_call x1, Pallas kernels, shards(): pl.pallas_call(kernel, out_shape=jax.ShapeDtypeStruct(residual.shape[::-1...  62.4 us
    unnamed x1, local copies, waits for them, and re-layouts  1.32 us

profile of v3, /device:TPU:1, one launch (start us, length us, event | category | flops | bytes accessed | tf_op | source)
XLA Modules:
  0.0 63.8 jit_solution(13105216190937173806)
XLA Ops:
  0.0 62.4 %cascade.1 = bf16[64,128]{1,0:T(8,128)(2,1)} custom-call(s32[8]{0:T(128)} %lengths_in.1, s32[8]{0:T(128)} %parents_in.1, bf16[8,1024]{1,0:T(8,128)(2,1)} %q_hbm.1, bf16[8,256]{1,0:T(8,128)(2,1)} %sk_hbm.1, bf16[8,256]{1,0:T(8,128)(2,1)} %sv_hbm.1, bf16[4096,256]{1,0:T(8,128)(2,1)} %pk_hbm.1, bf16[4096,256]{1,0:T(8,128)(2,1)} %pv_hbm.1, ...), custom_call_target="tpu_custom_call" | custom-call | flops 19327352832 | bytes 5242880 | tf_op jit(solution)/shard_map/cascade/pallas_call | solution.py:463
  62.5 1.3 %copy.11 = bf16[128,64]{0,1:T(8,128)(2,1)} copy(bf16[128,64]{0,1:T(8,128)(2,1)} %bitcast.3) | data formatting | bytes 32768

commit v4 on v3

--- a/solution.py
+++ b/solution.py
@@ -437,8 +437,8 @@
         sides.append((parts[0] + parts[1]) + (parts[2] + parts[3]))
     top = jnp.concatenate([sides[0][:, :64], sides[1][:, :64]], axis=1)
     bottom = jnp.concatenate([sides[0][:, 64:], sides[1][:, 64:]], axis=1)
-    out_ref[0:32, :] = (res_in[0:32, :].astype(F32) + top).astype(BF16)
-    out_ref[32:64, :] = (res_in[32:64, :].astype(F32) + bottom).astype(BF16)
+    state = res_in[...].astype(F32) + jnp.concatenate([top, bottom], axis=0)
+    out_ref[...] = state.T.astype(BF16)
 
     for g in range(2):
         wait_all(q.at[g, 0, pl.ds(0, NZ - 1)], qz_s.at[g])
@@ -460,9 +460,9 @@
 def shards(queries, suffix_keys, suffix_values, prefix_keys, prefix_values, lengths, parents, out_weight, residual):
     hbm = pl.BlockSpec(memory_space=pltpu.HBM)
     dma = pltpu.SemaphoreType.DMA
-    flipped = pl.pallas_call(
+    return pl.pallas_call(
         kernel,
-        out_shape=jax.ShapeDtypeStruct(residual.shape[::-1], BF16),
+        out_shape=jax.ShapeDtypeStruct(residual.shape, BF16),
         in_specs=[hbm] * 9,
         out_specs=pl.BlockSpec(memory_space=pltpu.VMEM),
         scratch_shapes=[
@@ -507,7 +507,6 @@
         ),
         name="cascade",
     )(lengths, parents, queries, suffix_keys, suffix_values, prefix_keys, prefix_values, out_weight.T, residual.T)
-    return flipped.T
 
 
 def solution(mesh):

time: 64 us -> 64.2 us (level)
    pallas_call x0 -> x1, local copies, waits for them, and re-layouts: none -> 1.45 us  [shards(): pl.pallas_call(kernel, out_shape=jax.ShapeDtypeStruct(residual.shape, BF1...]
    unnamed x1 -> x0, local copies, waits for them, and re-layouts: 1.32 us -> none
where the time goes in v4:
time: 64.2 us; the launch traced here: 64 us
  Pallas kernels  62.6 us (98%)
  local copies, waits for them, and re-layouts  1.45 us (2%)
    pallas_call x1, Pallas kernels, shards(): pl.pallas_call(kernel, out_shape=jax.ShapeDtypeStruct(residual.shape, BF1...  62.6 us
    pallas_call x1, local copies, waits for them, and re-layouts, shards(): pl.pallas_call(kernel, out_shape=jax.ShapeDtypeStruct(residual.shape, BF1...  1.45 us

profile of v4, /device:TPU:1, one launch (start us, length us, event | category | flops | bytes accessed | tf_op | source)
XLA Modules:
  0.0 64.0 jit_solution(12618883502188977463)
XLA Ops:
  0.0 62.6 %cascade.1 = bf16[128,64]{1,0:T(8,128)(2,1)} custom-call(s32[8]{0:T(128)} %lengths_in.1, s32[8]{0:T(128)} %parents_in.1, bf16[8,1024]{1,0:T(8,128)(2,1)} %q_hbm.1, bf16[8,256]{1,0:T(8,128)(2,1)} %sk_hbm.1, bf16[8,256]{1,0:T(8,128)(2,1)} %sv_hbm.1, bf16[4096,256]{1,0:T(8,128)(2,1)} %pk_hbm.1, bf16[4096,256]{1,0:T(8,128)(2,1)} %pv_hbm.1, ...), custom_call_target="tpu_custom_call" | custom-call | flops 19327352832 | bytes 5242880 | tf_op jit(solution)/shard_map/cascade/pallas_call | solution.py:463
  62.6 1.4 %copy.10 = bf16[128,64]{0,1:T(8,128)(2,1)} copy(bf16[128,64]{1,0:T(8,128)(2,1)} %cascade.1) | data formatting | bytes 32768 | tf_op jit(solution)/shard_map/cascade/pallas_call | solution.py:463
